TPU v7x, 32 devices: a whole 2x2x4 slice. The times are simulated.
32 devices in a mesh: dp: 8 (over y, x, core), ctx: 4 (over z).
Axes of the slice: x: 2, y: 2, z: 4, core: 2. Of those that a mesh axis runs over, the one named last changes fastest.
Arguments:
- cotangent: bfloat16 [8, 2048, 8192], P('dp', 'ctx'), may hold values from -6 to 6
- out_weight: bfloat16 [256, 8192], P(None, 'ctx'), may hold values from -0.0625 to 0.0625
- head_input: bfloat16 [8, 2048, 256], P('dp', 'ctx'), may hold values from -6 to 6
- injector: bfloat16 [8, 2048, 128], P('dp', 'ctx'), may hold values from -0.59765625 to 0.59765625
- readout: bfloat16 [8, 2048, 128], P('dp', 'ctx'), may hold values from -0.59765625 to 0.59765625
- decay_code: int32 [8, 2048, 2], P('dp', 'ctx'), may hold values from 1 to 20480
- decay_rate: float32 [2], replicated, may hold values from 9.765625e-06 to 0.012207031
- start_state: float32 [8, 4, 2, 128, 128], P('dp', 'ctx'), may hold values from -6 to 6
Outputs:
- gradient_input: bfloat16 [8, 2048, 256], P('dp', 'ctx')
- gradient_injector: float32 [8, 2048, 128], P('dp', 'ctx')
- gradient_readout: float32 [8, 2048, 128], P('dp', 'ctx')
- gradient_weight: float32 [256, 8192], P('ctx', 'dp')
- gradient_rate: float32 [2], replicated
All inputs are finite; a program needn't handle non-finite values.
Results may differ from a plain program's by a relative error of at most 0.0049.
Values may be sent and summed in bfloat16 or wider, within the bound.
A program may use at most 128 MiB of HBM per device.

v0:
```python
import jax
import jax.numpy as jnp
from jax import lax
from jax.sharding import PartitionSpec as P

precise = lax.Precision.HIGHEST


def carried_in(value, axis, join, neutral):
    count, mine = (lax.axis_size(axis), lax.axis_index(axis))
    pieces = jax.tree.map(lambda part: lax.all_gather(part, axis), value)
    pieces = jax.tree.map(lambda part: part[::-1], pieces)
    mine = count - 1 - mine
    total = jax.tree.map(
        lambda part, zero: jnp.full_like(part, 0) + jnp.asarray(zero, part.dtype), value, neutral
    )

    def lap(position, total):
        longer = join(total, jax.tree.map(lambda part: part[position], pieces))
        return jax.tree.map(lambda new, old: jnp.where(position < mine, new, old), longer, total)

    return lax.fori_loop(0, count - 1, lap, total)


def decay_table(log_decay):
    cumulative = jnp.cumsum(log_decay, axis=0)
    length = log_decay.shape[0]
    row_index = lax.broadcasted_iota(jnp.int32, (length, length), 0)
    col_index = lax.broadcasted_iota(jnp.int32, (length, length), 1)
    causal = (row_index >= col_index)[None]
    spread = cumulative.T[:, :, None] - cumulative.T[:, None, :]
    weights = jnp.where(causal, jnp.exp(jnp.where(causal, spread, 0.0)), 0.0)
    return (cumulative, weights)


def forward_shard(head_input, injector, readout, log_decay, start_state):
    length, heads_count = log_decay.shape
    cumulative, weights = decay_table(log_decay)
    intersection = jnp.dot(readout, injector.T, preferred_element_type=jnp.float32)
    mixing = intersection[None] * weights
    inputs_heads = head_input.reshape(length, heads_count, -1).astype(jnp.float32)
    within = jnp.einsum("hts,shp->thp", mixing, inputs_heads, precision=precise)
    carried = jnp.einsum("tn,hpn->thp", readout.astype(jnp.float32), start_state, precision=precise)
    outputs = within + jnp.exp(cumulative)[:, :, None] * carried
    return outputs.reshape(length, -1).astype(jnp.bfloat16)


def chain_piece(readout, output_grad, log_decay):
    length, heads_count = log_decay.shape
    cumulative = jnp.cumsum(log_decay, axis=0)
    grad_heads = output_grad.reshape(length, heads_count, -1).astype(jnp.float32)
    scaled = jnp.exp(cumulative)[:, :, None] * readout.astype(jnp.float32)[:, None, :]
    adjoint = jnp.einsum("thp,thn->hpn", grad_heads, scaled, precision=precise)
    return (jnp.exp(cumulative[-1]), adjoint)


def backward_shard(head_input, injector, readout, output_grad, log_decay, start_state, incoming):
    length, heads_count = log_decay.shape
    cumulative, weights = decay_table(log_decay)
    inputs_narrow = head_input.reshape(length, heads_count, -1)
    grad_narrow = output_grad.reshape(length, heads_count, -1)
    inputs_heads = inputs_narrow.astype(jnp.float32)
    grad_heads = grad_narrow.astype(jnp.float32)
    inject_float = injector.astype(jnp.float32)
    read_float = readout.astype(jnp.float32)
    intersection = jnp.dot(readout, injector.T, preferred_element_type=jnp.float32)
    mixing = intersection[None] * weights
    to_end = jnp.exp(cumulative[-1][None, :] - cumulative)
    from_start = jnp.exp(cumulative)
    entering = jnp.einsum("sn,hpn->shp", inject_float, incoming, precision=precise)
    grad_input = (
        jnp.einsum("hts,thp->shp", mixing, grad_heads, precision=precise)
        + to_end[:, :, None] * entering
    )
    pairing = (
        jnp.einsum("thp,shp->hts", grad_narrow, inputs_narrow, preferred_element_type=jnp.float32)
        * weights
    )
    through_start = jnp.einsum("thp,hpn->thn", grad_heads, start_state, precision=precise)
    grad_read = jnp.einsum("hts,sn->tn", pairing, inject_float, precision=precise)
    grad_read = grad_read + jnp.einsum("th,thn->tn", from_start, through_start, precision=precise)
    input_state = jnp.einsum("shp,hpn->shn", inputs_heads, incoming, precision=precise)
    grad_inject = jnp.einsum("hts,tn->sn", pairing, read_float, precision=precise)
    grad_inject = grad_inject + jnp.einsum("sh,shn->sn", to_end, input_state, precision=precise)
    products = intersection[None] * pairing
    carried = (
        jnp.einsum("tn,hpn->thp", read_float, start_state, precision=precise)
        * from_start[:, :, None]
    )
    reaching = to_end * jnp.einsum("shn,sn->sh", input_state, inject_float, precision=precise)
    end_term = from_start[-1] * jnp.einsum(
        "hpn,hpn->h", incoming, start_state, precision=precise
    ) + jnp.sum(reaching, axis=0)
    cumul_grad = jnp.sum(products, axis=2).T - jnp.sum(products, axis=1).T
    cumul_grad = cumul_grad + jnp.sum(grad_heads * carried, axis=2) - reaching
    is_last = lax.broadcasted_iota(jnp.int32, (length, 1), 0) == length - 1
    cumul_grad = cumul_grad + jnp.where(is_last, end_term[None, :], 0.0)
    decay_grad = jnp.flip(jnp.cumsum(jnp.flip(cumul_grad, 0), axis=0), 0)
    rate_terms = jnp.sum(decay_grad * log_decay, axis=0)
    return (grad_input.reshape(length, -1).astype(jnp.bfloat16), grad_inject, grad_read, rate_terms)


def combine(earlier, later):
    return (later[0] * earlier[0], later[1] + later[0][:, None, None] * earlier[1])


def local(
    cotangent, out_weight, head_input, injector, readout, decay_code, decay_rate, start_state
):
    grad_out = cotangent[0]
    inputs_local = head_input[0]
    inject_local = injector[0]
    read_local = readout[0]
    state_local = start_state[0, 0]
    length = grad_out.shape[0]
    output_grad = lax.dot_general(
        grad_out,
        lax.all_gather(out_weight, "ctx", axis=1, tiled=True),
        (((1,), (1,)), ((), ())),
        preferred_element_type=jnp.float32,
    ).astype(jnp.bfloat16)
    log_decay = -decay_rate[None, :] * decay_code[0].astype(jnp.float32)
    decay_total, adjoint = chain_piece(read_local, output_grad, log_decay)
    identity = (jnp.ones_like(decay_total), jnp.zeros_like(adjoint))
    incoming = carried_in((decay_total, adjoint), "ctx", combine, identity)[1]
    outputs = forward_shard(inputs_local, inject_local, read_local, log_decay, state_local)
    local_weight = lax.dot_general(
        outputs, grad_out, (((0,), (0,)), ((), ())), preferred_element_type=jnp.float32
    )
    data_part = lax.psum_scatter(local_weight, "dp", scatter_dimension=1, tiled=True)
    weight_part = lax.psum_scatter(data_part, "ctx", scatter_dimension=0, tiled=True)
    grad_input, grad_inject, grad_read, rate_terms = backward_shard(
        inputs_local, inject_local, read_local, output_grad, log_decay, state_local, incoming
    )
    tokens_all = length * lax.axis_size("dp") * lax.axis_size("ctx")
    rate_sum = lax.psum(rate_terms, ("dp", "ctx"))
    return (
        grad_input[None],
        grad_inject[None],
        grad_read[None],
        weight_part,
        rate_sum / tokens_all,
    )


def solution(mesh):
    in_specs = (
        P("dp", "ctx", None),
        P(None, "ctx"),
        P("dp", "ctx", None),
        P("dp", "ctx", None),
        P("dp", "ctx", None),
        P("dp", "ctx", None),
        P(),
        P("dp", "ctx", None, None, None),
    )
    out_specs = (
        P("dp", "ctx", None),
        P("dp", "ctx", None),
        P("dp", "ctx", None),
        P("ctx", "dp"),
        P(),
    )
    return jax.shard_map(local, mesh=mesh, in_specs=in_specs, out_specs=out_specs, check_vma=False)
```

profile of v0, /device:TPU:9, one launch (start us, length us, event | category | flops | bytes accessed | tf_op | source)
XLA Modules:
  0.0 241.9 jit_solution(1334961983964797294)
XLA Ops:
  7.2 0.0 all-gather.4.cloned.1.call-start
  7.2 0.7 all-gather.4.cloned.1.call-update
  7.9 0.0 reduce-scatter.3.cloned.1.call-start
  7.9 0.7 neg.4
  8.6 0.8 fusion.61
  9.4 0.6 reduce-window.14
  10.0 0.2 slice_reduce_fusion.1
  10.1 0.2 reduce-window.15
  10.3 0.1 add_bitcast_fusion.1
  10.4 1.1 copy.91
  11.5 0.0 copy-start.3
  11.5 0.1 iota_compare_fusion
  11.6 0.0 copy-start.4
  11.6 1.3 fusion.55
  13.0 0.0 copy-start.1
  13.0 0.0 copy-start.2
  13.0 76.0 %all-gather.4.cloned.1.call-done = bf16[256,8192]{1,0:T(8,128)(2,1)} async-done(((bf16[256,2048]{1,0:T(8,128)(2,1)}), bf16[256,8192]{1,0:T(8,128)(2,1)}) %all-gather.4.cloned.1.call-update) | async-done | bytes 4194320 | tf_op jit(solution)/shard_map/all_gather | solution.py:118
  89.0 6.9 %fusion.26 = bf16[512,256]{0,1:T(8,128)(2,1)S(1)} fusion(bf16[256,8192]{1,0:T(8,128)(2,1)} %all-gather.4.cloned.1.call-done, bf16[1,512,8192]{2,1,0:T(8,128)(2,1)} %param.10), kind=kOutput, calls=%fused_computation.24 | convolution fusion | flops 2147614720 | bytes 12845056 | tf_op jit(solution)/shard_map/dot_general | solution.py:116
  96.0 0.4 multiply_reduce_fusion.2
  96.4 2.0 fusion.22
  98.4 9.1 %fusion.1 = f32[256,8192]{1,0:T(8,128)} fusion(bf16[512,256]{0,1:T(8,128)(2,1)S(1)} %bitcast.164, bf16[1,512,8192]{2,1,0:T(8,128)(2,1)} %param.10), kind=kOutput, calls=%fused_computation.3 | convolution fusion | flops 2147483648 | bytes 17039360 | tf_op jit(solution)/shard_map/dot_general | solution.py:127
  107.5 0.0 reduce-scatter.3.cloned.1.call-update
  107.5 0.0 reduce-scatter.5.cloned.1.call-start
  107.5 0.2 slice_reduce_fusion.3
  107.7 8.6 %all-gather.1 = f32[4,1,2]{2,1,0:T(1,128)S(1)} all-gather(f32[1,1,2]{2,1,0:T(1,128)S(1)} %bitcast.175), channel_id=1, replica_groups=mesh['dp'=8,'ctx'=4] {'ctx'}, dimensions={0}, use_global_device_ids=true | all-gather | bytes 40 | tf_op jit(solution)/shard_map/all_gather | solution.py:11
  116.3 0.1 copy.54
  116.4 0.1 rev.14
  116.5 0.1 copy.55
  116.6 0.8 copy.89
  117.5 0.1 copy.52
  117.6 0.2 slice_reduce_fusion.2
  117.8 0.4 fusion.43
  118.2 11.2 %all-gather = f32[8,128,128]{2,1,0:T(8,128)S(1)} all-gather(f32[2,128,128]{2,1,0:T(8,128)S(1)} %fusion.43), channel_id=2, replica_groups=mesh['dp'=8,'ctx'=4] {'ctx'}, dimensions={0}, use_global_device_ids=true | all-gather | bytes 655360 | tf_op jit(solution)/shard_map/all_gather | solution.py:11
  129.5 0.4 while.14
  129.5 0.1 fusion.81
  129.6 0.1 fusion.81
  129.8 0.1 fusion.81
  129.9 0.1 fusion.49
  130.0 1.5 fusion.41
  131.5 0.2 multiply_reduce_fusion.4
  131.7 0.0 copy-start.6
  131.7 2.3 multiply_reduce_fusion
  134.0 0.1 fusion.60
  134.0 0.4 rev.15
  134.4 0.6 reduce-window.16
  135.0 45.0 %reduce-scatter.3.cloned.1.call-done = f32[256,1024]{1,0:T(8,128)} async-done(((f32[256,8192]{1,0:T(8,128)}), f32[256,1024]{1,0:T(8,128)}) %reduce-scatter.3.cloned.1.call-update) | async-done | bytes 1048592 | tf_op jit(solution)/shard_map/reduce_scatter | solution.py:130
  180.0 0.0 reduce-scatter.5.cloned.1.call-update
  180.0 0.2 slice_reduce_fusion
  180.2 0.2 reduce-window.19
  180.4 0.1 add_bitcast_fusion
  180.4 0.4 rev.16
  180.8 0.2 multiply_reduce_fusion.3
  181.0 0.9 copy.72
  181.8 40.2 %psum.7 = f32[2]{0:T(128)S(1)} all-reduce(f32[2]{0:T(128)S(1)} %multiply_reduce_fusion.3), channel_id=1, replica_groups=mesh['dp'=8,'ctx'=4] {'dp','ctx'}, use_global_device_ids=true, to_apply=%region_14.15 | all-reduce | flops 2 | bytes 16 | tf_op jit(solution)/shard_map/psum | solution.py:136
  222.1 0.8 fusion.42
  222.8 1.1 copy.70
  223.9 2.5 %fusion.11 = f32[512,2,128]{0,2,1:T(8,128)S(1)} fusion(bf16[512,2,128]{0,2,1:T(8,128)(2,1)S(1)} %bitcast.157, f32[2,512]{1,0:T(2,128)S(1)} %bitcast.171, f32[512,512]{1,0:T(8,128)S(1)} %fusion.55, pred[512,512]{1,0:T(8,128)(4,1)} %copy-done.4), kind=kOutput, calls=%fused_computation.14 | convolution fusion | flops 807403520 | bytes 2101248 | tf_op jit(solution)/shard_map/hts,thp->shp/dot_general | solution.py:72
  226.4 0.4 fusion.25
  226.8 0.8 copy.62
  227.7 0.4 convolution_bitcast_fusion
  228.1 3.7 %fusion.45 = f32[512,1,128]{2,1,0:T(1,128)S(1)} fusion(f32[512,2,1]{1,2,0:T(1,128)S(1)} %copy-done.5, f32[512,2,128]{2,0,1:T(8,128)S(1)} %convolution_bitcast_fusion), kind=kOutput, calls=%fused_computation.47 | convolution fusion | flops 1572864 | bytes 790528 | tf_op jit(solution)/shard_map/th,thn->tn/dot_general | solution.py:81
  231.8 1.3 fusion.29
  233.2 1.7 fusion.30
  234.9 0.5 broadcast_multiply_fusion
  (24 shorter events, 0.2 us)
Async XLA Ops:
  7.2 81.8 %all-gather.4.cloned.1.call-start = ((), (), s32[]{:S(2)}) async-start(), calls=%async_computation.2 | async-start | bytes 5242880 | tf_op jit(solution)/shard_map/all_gather | solution.py:118
  7.9 172.1 %reduce-scatter.3.cloned.1.call-start = ((), (), s32[]{:S(2)}) async-start(), calls=%async_computation.3 | async-start | bytes 9437184 | tf_op jit(solution)/shard_map/reduce_scatter | solution.py:130
  11.5 84.9 %copy-start.3 = (bf16[1,512,256]{1,2,0:T(8,128)(2,1)}, bf16[1,512,256]{1,2,0:T(8,128)(2,1)S(1)}, u32[]{:S(2)}) copy-start(bf16[1,512,256]{1,2,0:T(8,128)(2,1)S(1)} %copy.91) | copy-start | bytes 786436
  11.6 84.8 %copy-start.4 = (pred[512,512]{1,0:T(8,128)(4,1)}, pred[512,512]{1,0:T(8,128)(4,1)S(1)}, u32[]{:S(2)}) copy-start(pred[512,512]{1,0:T(8,128)(4,1)S(1)} %iota_compare_fusion) | copy-start | bytes 786436
  13.0 83.0 %copy-start.1 = (bf16[1,512,128]{2,1,0:T(8,128)(2,1)S(1)}, bf16[1,512,128]{2,1,0:T(8,128)(2,1)}, u32[]{:S(2)}) copy-start(bf16[1,512,128]{2,1,0:T(8,128)(2,1)} %param.14) | copy-start | bytes 393220
  13.0 83.0 %copy-start.2 = (f32[1,1,2,128,128]{4,3,2,1,0:T(8,128)S(1)}, f32[1,1,2,128,128]{4,3,2,1,0:T(8,128)}, u32[]{:S(2)}) copy-start(f32[1,1,2,128,128]{4,3,2,1,0:T(8,128)} %param.17) | copy-start | bytes 393220
  107.5 9.1 %copy-start = (bf16[1,512,128]{2,1,0:T(8,128)(2,1)S(1)}, bf16[1,512,128]{2,1,0:T(8,128)(2,1)}, u32[]{:S(2)}) copy-start(bf16[1,512,128]{2,1,0:T(8,128)(2,1)} %param.13) | copy-start | bytes 393220
  107.5 127.9 %reduce-scatter.5.cloned.1.call-start = ((), (), s32[]{:S(2)}) async-start(), calls=%async_computation.4 | async-start | bytes 1310720 | tf_op jit(solution)/shard_map/reduce_scatter | solution.py:131
  131.7 49.1 %copy-start.6 = (s32[1,512,2]{1,2,0:T(2,128)S(1)}, s32[1,512,2]{1,2,0:T(2,128)}, u32[]{:S(2)}) copy-start(s32[1,512,2]{1,2,0:T(2,128)} %param.15) | copy-start | bytes 12292
  226.4 1.7 copy-start.5
Sparse Core Ops, SparseCore 0:
  9.6 79.3 all-gather.3
  107.6 72.3 reduce-scatter.2
  183.0 25.8 reduce-scatter.4
where the time goes:
time: 244 us; the launch traced here: 242 us
  waiting for transfers between devices  122 us (50%)
  blocking collectives  60 us (25%)
  matrix products  34 us (14%)
  between operations  14 us (6%)
  local copies, waits for them, and re-layouts  6.65 us (3%)
  other arithmetic  5.37 us (2%)
    all_gather x1, waiting for transfers between devices, local(): lax.all_gather(out_weight, 'ctx', axis=1, tiled=True)  76 us
    reduce_scatter x1, waiting for transfers between devices, local(): lax.psum_scatter(local_weight, 'dp', scatter_dimension=1, tiled=True)  45 us
    psum x1, blocking collectives, local(): rate_sum = lax.psum(rate_terms, ('dp', 'ctx'))  40.2 us
    all_gather x2, blocking collectives, carried_in(): pieces = jax.tree.map(lambda part: lax.all_gather(part, axis), value)  19.8 us
    dot_general x1, matrix products, local(): lax.dot_general(outputs, grad_out, (((0,), (0,)), ((), ())), preferred_el...  9.06 us
    dot_general x1, matrix products, local(): lax.dot_general(grad_out, lax.all_gather(out_weight, 'ctx', axis=1, tiled...  6.93 us
  transfers between devices with their start and end apart: 3, of which 2 were waited for; matrix products, arithmetic and copies ran while one was open for 11% of the time, Pallas kernels for 0%

commit v1 on v0

v1 whole, which is shorter than its diff:
```python
import functools

import jax
import jax.numpy as jnp
from jax import lax
from jax.experimental import pallas as pl
from jax.experimental.pallas import tpu as pltpu
from jax.sharding import PartitionSpec as P

F32, BF16 = jnp.float32, jnp.bfloat16
MESH = pl.DeviceIdType.MESH


def nn(a, b):
    return lax.dot_general(a, b, (((1,), (0,)), ((), ())), preferred_element_type=F32)


def nt(a, b):
    return lax.dot_general(a, b, (((1,), (1,)), ((), ())), preferred_element_type=F32)


def halves(value):
    high = value.astype(BF16)
    return high, (value - high.astype(F32)).astype(BF16)


def fold(row):
    total = row[:, :128]
    for at in range(128, row.shape[1], 128):
        total = total + row[:, at : at + 128]
    return total


def kernel(
    n, dps,
    rate_ref, cot_hbm, w_ref, x_ref, inj_ref, read_ref, codecol_ref, coderow_ref, start_ref,
    gi_ref, ginj_ref, gread_ref, gw_ref, rate_out,
    cot, wslot, acc, own, part_send, part_recv, plane_send, plane_recv, zsend, zrecv,
    fwd_t, mix_t, wts, wts_t, qts, scal, inc, chain_send, rate_z, rate_dp, rate_mine, rate_mid,
    cot_sem, send_sem, zsem, psem, csem, asem, bsem, dsem, chsem, r1sem, r2sem,
):
    length, heads = x_ref.shape[0], start_ref.shape[0]
    dz = w_ref.shape[1]
    chips = dps // 2
    rows, cols = gw_ref.shape
    dp, c = lax.axis_index("dp"), lax.axis_index("ctx")
    chip, core = lax.div(dp, 2), lax.rem(dp, 2)
    partner = (chip * 2 + 1 - core, c)
    quarter = w_ref.shape[0] // 4
    sent = []
    counter = [0]

    def send(src, dst, recv_sem, device, cond=None):
        index = counter[0]
        counter[0] += 1
        copy = pltpu.make_async_remote_copy(
            src_ref=src, dst_ref=dst, send_sem=send_sem.at[index], recv_sem=recv_sem,
            device_id=device, device_id_type=MESH,
        )
        sent.append((copy, cond))
        if cond is None:
            copy.start()
        else:
            pl.when(cond)(lambda: copy.start())

    def arrived(dst, recv_sem):
        pltpu.make_async_copy(dst, dst, recv_sem).wait()

    loads = []
    for i in range(4):
        r = pl.ds(i * (length // 4), length // 4)
        load = pltpu.make_async_copy(cot_hbm.at[r], cot.at[r], cot_sem.at[i])
        load.start()
        loads.append(load)

    barrier = pltpu.get_barrier_semaphore()
    for i in range(1, dps):
        pl.semaphore_signal(barrier, inc=1, device_id=(lax.rem(dp + i, dps), c), device_id_type=MESH)
    for i in range(1, n):
        pl.semaphore_signal(barrier, inc=1, device_id=(dp, lax.rem(c + i, n)), device_id_type=MESH)
    pl.semaphore_wait(barrier, dps + n - 2)

    def shard_place(shard):
        par = lax.rem(shard, 2)
        bit = lax.rem(chip, 2) * (1 - par) + lax.rem(lax.div(chip, 2), 2) * par
        peer = chip + (1 - 2 * bit) * (1 + par)
        return bit, peer

    def q_rows(k, bit):
        return pl.ds(pl.multiple_of((2 * k + bit) * quarter, quarter), quarter)

    bit, _ = shard_place(c)
    mine = q_rows(core, bit)
    send(w_ref.at[mine], wslot.at[0, 0, mine], zsem.at[0, 0], (dp, lax.rem(c + 1, n)), c + 1 < n)
    send(w_ref.at[mine], wslot.at[1, 0, mine], zsem.at[1, 0], (dp, lax.rem(c + n - 1, n)), c > 0)

    def shard_of(way, step):
        return (c - 1 - step, c - 1 - step >= 0) if way == 0 else (c + 1 + step, c + 1 + step < n)

    def w_z(step):
        for way in range(2):
            shard, valid = shard_of(way, step)
            shard = lax.rem(shard + n, n)
            bit, peer = shard_place(shard)
            here = q_rows(core, bit)
            slot = wslot.at[way, step, here]
            pl.when(valid)(lambda: arrived(slot, zsem.at[way, step]))
            if step + 1 < n - 1:
                if way == 0:
                    send(slot, wslot.at[way, step + 1, here], zsem.at[way, step + 1],
                         (dp, lax.rem(c + 1, n)), valid & (c + 1 < n))
                else:
                    send(slot, wslot.at[way, step + 1, here], zsem.at[way, step + 1],
                         (dp, lax.rem(c + n - 1, n)), valid & (c > 0))
            send(slot, slot, psem.at[way, step], (peer * 2 + core, c), valid)
            send(slot, slot, csem.at[way, step, 0], partner, valid)

    def w_plane(step):
        for way in range(2):
            shard, valid = shard_of(way, step)
            shard = lax.rem(shard + n, n)
            bit, _ = shard_place(shard)
            slot = wslot.at[way, step, q_rows(core, 1 - bit)]
            pl.when(valid)(lambda: arrived(slot, psem.at[way, step]))
            send(slot, slot, csem.at[way, step, 1], partner, valid)

    def w_use(step):
        for way in range(2):
            shard, valid = shard_of(way, step)
            shard = lax.rem(shard + n, n)
            bit, _ = shard_place(shard)

            @pl.when(valid)
            def _():
                for which in range(2):
                    there = bit if which == 0 else 1 - bit
                    arrived(wslot.at[way, step, q_rows(1 - core, there)], csem.at[way, step, which])
                at = pl.ds(pl.multiple_of(shard * dz, dz), dz)
                acc[...] += nt(cot[:, at], wslot[way, step])

    row_at = lax.broadcasted_iota(jnp.int32, (length, length), 0)
    col_at = lax.broadcasted_iota(jnp.int32, (length, length), 1)
    lower = row_at >= col_at
    upper = col_at >= row_at
    col_sum = nn(jnp.where(lower, 1.0, 0.0).astype(BF16), codecol_ref[...])
    row_sum = nn(coderow_ref[...], jnp.where(upper, 1.0, 0.0).astype(BF16))
    inter_t = nt(inj_ref[...], read_ref[...])
    x_t = x_ref[...].astype(F32).T.astype(BF16)
    cum_col, cum_row = [], []
    for h in range(heads):
        ch = slice(h * 128, (h + 1) * 128)
        rate = rate_ref[h]
        cc = -rate * (256.0 * col_sum[:, h : h + 1] + col_sum[:, heads + h : heads + h + 1])
        cr = -rate * (256.0 * row_sum[h : h + 1] + row_sum[heads + h : heads + h + 1])
        cum_col.append(cc)
        cum_row.append(cr)
        w_t = jnp.where(upper, jnp.exp(jnp.where(upper, cr - cc, 0.0)), 0.0)
        wts_t[h] = w_t
        mixed = (inter_t * w_t).astype(BF16)
        mix_t[h] = mixed
        high, low = halves(start_ref[h])
        carried = nt(high, read_ref[...]) + nt(low, read_ref[...])
        fwd_t[ch, :] = (nn(x_t[ch], mixed) + jnp.exp(cr) * carried).astype(BF16)

    for load in loads:
        load.wait()

    def block(chip_at, core_at):
        at = pl.ds(pl.multiple_of((chip_at * 2 + core_at) * cols, cols), cols)
        return nn(fwd_t[...], cot[:, at])

    order = list(range(1, chips)) + [0]
    for i in order:
        target = lax.rem(chip + i, chips)
        part_send[i] = block(target, 1 - core).astype(BF16)
        send(part_send.at[i], part_recv.at[i], asem.at[i], partner)
    w_z(0)
    for i in order:
        target = lax.rem(chip + i, chips)
        own[i] = block(target, core)
        arrived(part_recv.at[i], asem.at[i])
        if i:
            plane_send[i - 1] = (own[i] + part_recv[i].astype(F32)).astype(BF16)
            send(plane_send.at[i - 1], plane_recv.at[i - 1], bsem.at[i - 1], (target * 2 + core, c))
        else:
            own[0] = own[0] + part_recv[0].astype(F32)

    acc[...] = nt(cot[:, pl.ds(pl.multiple_of(c * dz, dz), dz)], w_ref[...])
    w_plane(0)
    for step in range(1, n - 1):
        w_z(step)
        if step == 1:
            inter = nt(read_ref[...], inj_ref[...])
            for h in range(heads):
                spread = jnp.where(lower, cum_col[h] - cum_row[h], 0.0)
                weight = jnp.where(lower, jnp.exp(spread), 0.0)
                wts[h] = weight
                qts[h] = inter * weight * spread
                high, low = halves(jnp.exp(cum_col[h]) * read_ref[...].astype(F32))
                scal[h, :, :128] = high
                scal[h, :, 128:] = low
        w_use(step - 1)
        w_plane(step)
    w_use(n - 2)

    grad = acc[...].astype(BF16)
    grad_t = grad.astype(F32).T.astype(BF16)
    last = [cum_col[h][length - 1 : length, :] for h in range(heads)]
    pieces = []
    for h in range(heads):
        both = nn(grad_t[h * 128 : (h + 1) * 128], scal[h])
        pieces.append(both[:, :128] + both[:, 128:])
    before = (dp, lax.rem(c + n - 1, n))

    @pl.when(c == n - 1)
    def _():
        inc[...] = jnp.zeros_like(inc)

    for h in range(heads):
        chain_send[h] = pieces[h]
        send(chain_send.at[h], inc.at[h], chsem.at[h], before, c == n - 1)

    inject, read = inj_ref[...], read_ref[...]
    pair = pair_t = None
    rates = []
    through_sum = None
    for h in range(heads):
        ch = slice(h * 128, (h + 1) * 128)
        raw = nt(grad[:, ch], x_ref[:, ch])
        raw_t = nt(x_ref[:, ch], grad[:, ch])
        one, one_t = raw * wts[h], raw_t * wts_t[h]
        pair = one if pair is None else pair + one
        pair_t = one_t if pair_t is None else pair_t + one_t
        rate_row = fold(jnp.sum(raw * qts[h], axis=0, keepdims=True))
        high, low = halves(start_ref[h])
        through = jnp.exp(cum_col[h]) * (nn(grad[:, ch], high) + nn(grad[:, ch], low))
        through_sum = through if through_sum is None else through_sum + through
        rate_row = rate_row + jnp.sum(cum_col[h] * (through * read.astype(F32)), axis=0, keepdims=True)
        rates.append(rate_row)
    gread_ref[...] = nn(pair.astype(BF16), inject) + through_sum
    ginj_ref[...] = nn(pair_t.astype(BF16), read)

    for h in range(heads):
        @pl.when(c < n - 1)
        def _():
            arrived(inc.at[h], chsem.at[h])

        @pl.when((c < n - 1) & (c > 0))
        def _():
            chain_send[h] = chain_send[h] + jnp.exp(last[h]) * inc[h]

        send(chain_send.at[h], inc.at[h], chsem.at[h], before, (c < n - 1) & (c > 0))

    for i in range(chips - 1):
        arrived(plane_recv.at[i], bsem.at[i])
        own[0] = own[0] + plane_recv[i].astype(F32)
    for i in range(1, n):
        target = lax.rem(c + i, n)
        at = pl.ds(pl.multiple_of(target * rows, rows), rows)
        zsend[i - 1] = own[0, at, :].astype(BF16)
        send(zsend.at[i - 1], zrecv.at[i - 1], dsem.at[i - 1], (dp, target))

    rate_mine[...] = jnp.zeros_like(rate_mine)
    ginj = ginj_ref[...]
    for h in range(heads):
        ch = slice(h * 128, (h + 1) * 128)
        left = last[h] - cum_col[h]
        to_end = jnp.exp(left)
        high, low = halves(inc[h])
        entering = to_end * nt(inject, high)
        gi_ref[:, ch] = (nn(mix_t[h], grad[:, ch]) + entering).astype(BF16)
        reach = to_end * (nn(x_ref[:, ch], high) + nn(x_ref[:, ch], low))
        ginj = ginj + reach
        row = rates[h] + jnp.sum(left * (reach * inject.astype(F32)), axis=0, keepdims=True)
        row = row + (jnp.exp(last[h]) * last[h]) * jnp.sum(inc[h] * start_ref[h], axis=0, keepdims=True)
        rate_mine[h : h + 1, :] = row
    ginj_ref[...] = ginj

    for i in range(1, n):
        send(rate_mine, rate_z.at[i - 1], r1sem.at[i - 1], (dp, lax.rem(c + i, n)))
    total = rate_mine[...]
    for i in range(n - 1):
        arrived(rate_z.at[i], r1sem.at[i])
        total = total + rate_z[i]
    rate_mid[...] = total
    for i in range(1, dps):
        send(rate_mid, rate_dp.at[i - 1], r2sem.at[i - 1], (lax.rem(dp + i, dps), c))

    at = pl.ds(pl.multiple_of(c * rows, rows), rows)
    result = own[0, at, :]
    for i in range(n - 1):
        arrived(zrecv.at[i], dsem.at[i])
        result = result + zrecv[i].astype(F32)
    gw_ref[...] = result

    for i in range(dps - 1):
        arrived(rate_dp.at[i], r2sem.at[i])
        total = total + rate_dp[i]
    rate_out[...] = total

    for copy, cond in sent:
        if cond is None:
            copy.wait_send()
        else:
            pl.when(cond)(lambda: copy.wait_send())


def local(n, dps, cotangent, out_weight, head_input, injector, readout, decay_code, decay_rate, start_state):
    length, width = cotangent.shape[1:]
    channels, dz = out_weight.shape
    heads = decay_rate.shape[0]
    chips = dps // 2
    rows, cols = channels // n, width // dps
    code = decay_code[0]
    parts = jnp.concatenate([code // 256, code % 256], axis=1).astype(BF16)
    code_col = jnp.pad(parts, ((0, 0), (0, 128 - 2 * heads)))
    code_row = jnp.pad(parts.T, ((0, 16 - 2 * heads), (0, 0)))
    sends = 2 + 2 * (n - 2) + 6 * (n - 1) + chips + (chips - 1) + 2 * heads + 2 * (n - 1) + (dps - 1)
    vmem = pl.BlockSpec(memory_space=pltpu.VMEM)
    dma = pltpu.SemaphoreType.DMA
    gi, ginj, gread, gw, rate = pl.pallas_call(
        functools.partial(kernel, n, dps),
        out_shape=(
            jax.ShapeDtypeStruct((length, channels), BF16),
            jax.ShapeDtypeStruct((length, 128), F32),
            jax.ShapeDtypeStruct((length, 128), F32),
            jax.ShapeDtypeStruct((rows, cols), F32),
            jax.ShapeDtypeStruct((8, 128), F32),
        ),
        in_specs=[pl.BlockSpec(memory_space=pltpu.SMEM), pl.BlockSpec(memory_space=pl.ANY)] + [vmem] * 7,
        out_specs=(vmem,) * 5,
        scratch_shapes=[
            pltpu.VMEM((length, width), BF16),
            pltpu.VMEM((2, n - 1, channels, dz), BF16),
            pltpu.VMEM((length, channels), F32),
            pltpu.VMEM((chips, channels, cols), F32),
            pltpu.VMEM((chips, channels, cols), BF16),
            pltpu.VMEM((chips, channels, cols), BF16),
            pltpu.VMEM((chips - 1, channels, cols), BF16),
            pltpu.VMEM((chips - 1, channels, cols), BF16),
            pltpu.VMEM((n - 1, rows, cols), BF16),
            pltpu.VMEM((n - 1, rows, cols), BF16),
            pltpu.VMEM((channels, length), BF16),
            pltpu.VMEM((heads, length, length), BF16),
            pltpu.VMEM((heads, length, length), F32),
            pltpu.VMEM((heads, length, length), F32),
            pltpu.VMEM((heads, length, length), F32),
            pltpu.VMEM((heads, length, 256), BF16),
            pltpu.VMEM((heads, 128, 128), F32),
            pltpu.VMEM((heads, 128, 128), F32),
            pltpu.VMEM((n - 1, 8, 128), F32),
            pltpu.VMEM((dps - 1, 8, 128), F32),
            pltpu.VMEM((8, 128), F32),
            pltpu.VMEM((8, 128), F32),
            dma((4,)),
            dma((sends,)),
            dma((2, n - 1)),
            dma((2, n - 1)),
            dma((2, n - 1, 2)),
            dma((chips,)),
            dma((chips - 1,)),
            dma((n - 1,)),
            dma((heads,)),
            dma((n - 1,)),
            dma((dps - 1,)),
        ],
        compiler_params=pltpu.CompilerParams(
            collective_id=0, has_side_effects=True, vmem_limit_bytes=60 * 1024 * 1024
        ),
        cost_estimate=pl.CostEstimate(flops=10**10, bytes_accessed=2 * 10**7, transcendentals=10**6),
    )(
        decay_rate, cotangent[0], out_weight, head_input[0], injector[0], readout[0],
        code_col, code_row, start_state[0, 0],
    )
    tokens_all = length * dps * n
    return gi[None], ginj[None], gread[None], gw, jnp.sum(rate, axis=1)[:heads] / tokens_all


def solution(mesh):
    n, dps = mesh.shape["ctx"], mesh.shape["dp"]
    in_specs = (
        P("dp", "ctx", None),
        P(None, "ctx"),
        P("dp", "ctx", None),
        P("dp", "ctx", None),
        P("dp", "ctx", None),
        P("dp", "ctx", None),
        P(),
        P("dp", "ctx", None, None, None),
    )
    out_specs = (
        P("dp", "ctx", None),
        P("dp", "ctx", None),
        P("dp", "ctx", None),
        P("ctx", "dp"),
        P(),
    )
    return jax.shard_map(
        functools.partial(local, n, dps), mesh=mesh, in_specs=in_specs, out_specs=out_specs, check_vma=False
    )
```

time: 244 us -> 98.2 us (0.40)
  waiting for transfers between devices: 122 us -> 0 us
  Pallas kernels: 0 us -> 87 us
  blocking collectives: 60 us -> 0 us
  matrix products: 34 us -> 0 us
  between operations: 14 us -> 0.66 us
  other arithmetic: 5.37 us -> 2.03 us
    pallas_call x0 -> x1, Pallas kernels: none -> 87 us  [local(): pl.pallas_call(functools.partial(kernel, n, dps), out_shape=(jax.ShapeDty...]
    all_gather x1 -> x0, waiting for transfers between devices: 76 us -> none  [local(): lax.all_gather(out_weight, 'ctx', axis=1, tiled=True)]
    reduce_scatter x2 -> x0, waiting for transfers between devices: 45 us -> none  [the longest x1 45 us: local(): lax.psum_scatter(local_weight, 'dp', scatter_dimension=1, tiled=True)]
    psum x1 -> x0, blocking collectives: 40.2 us -> none  [local(): rate_sum = lax.psum(rate_terms, ('dp', 'ctx'))]
    dot_general x14 -> x0, matrix products: 34 us -> none  [the longest x1 9.06 us: local(): lax.dot_general(outputs, grad_out, (((0,), (0,)), ((), ())), preferred_el...]
    all_gather x2 -> x0, blocking collectives: 19.8 us -> none  [carried_in(): pieces = jax.tree.map(lambda part: lax.all_gather(part, axis), value)]
    unnamed x19 -> x5, local copies, waits for them, and re-layouts: 1.83 us -> 6.85 us
  transfers between devices with their start and end apart: 3 -> 0, of which waited for: 2 -> 0; matrix products, arithmetic and copies ran while one was open for 11% -> 0% of each run, Pallas kernels for 0% -> 0%
where the time goes in v1:
time: 98.2 us; the launch traced here: 97.8 us
  Pallas kernels  87 us (89%)
  local copies, waits for them, and re-layouts  8.15 us (8%)
  other arithmetic  2.03 us (2%)
    pallas_call x1, Pallas kernels, local(): pl.pallas_call(functools.partial(kernel, n, dps), out_shape=(jax.ShapeDty...  87 us
    unnamed x5, local copies, waits for them, and re-layouts  6.85 us

profile of v1, /device:TPU:9, one launch (start us, length us, event | category | flops | bytes accessed | tf_op | source)
XLA Modules:
  0.0 97.8 jit_solution(17043452047078771654)
XLA Ops:
  0.6 0.7 fusion.1
  1.4 0.6 pad.9.coderow_ref
  2.0 0.2 copy.14
  2.2 0.7 pad.8.clone.codecol_ref
  2.8 87.0 %shard_map.119 = (bf16[512,256]{1,0:T(8,128)(2,1)}, f32[512,128]{1,0:T(8,128)}, f32[512,128]{1,0:T(8,128)}, f32[64,1024]{1,0:T(8,128)}, f32[8,128]{1,0:T(8,128)}) custom-call(f32[2]{0:T(128)} %rate_ref.1, bf16[512,8192]{1,0:T(8,128)(2,1)} %bitcast.35, bf16[256,2048]{1,0:T(8,128)(2,1)} %w_ref.1, bf16[512,256]{1,0:T(8,128)(2,1)} %bitcast.36, ...), custom_call_target="tpu_custom_call" | custom-call | flops 10000000000 | bytes 20000000 | tf_op jit(solution)/shard_map/pallas_call | solution.py:321
  89.8 0.8 reduce_sum.9
  90.6 0.5 slice_multiply_fusion
  91.2 1.7 %copy.19 = bf16[1,512,256]{2,1,0:T(8,128)(2,1)} copy(bf16[1,512,256]{2,1,0:T(8,128)(2,1)} %bitcast.34) | data formatting | bytes 524288
  92.8 1.7 %copy.20 = f32[1,512,128]{2,1,0:T(8,128)} copy(f32[1,512,128]{2,1,0:T(8,128)} %bitcast.33) | data formatting | bytes 524288
  94.5 1.7 %copy.21 = f32[1,512,128]{2,1,0:T(8,128)} copy(f32[1,512,128]{2,1,0:T(8,128)} %bitcast.32) | data formatting | bytes 524288
  96.2 1.7 %copy.22 = f32[64,1024]{1,0:T(8,128)} copy(f32[64,1024]{1,0:T(8,128)} %get-tuple-element.27) | data formatting | bytes 524288
  (1 shorter events, 0.0 us)

commit v2 on v1

--- a/solution.py
+++ b/solution.py
@@ -33,7 +33,7 @@
 
 def kernel(
     n, dps,
-    rate_ref, cot_hbm, w_ref, x_ref, inj_ref, read_ref, codecol_ref, coderow_ref, start_ref,
+    rate_ref, cot_hbm, w_ref, x_ref, inj_ref, read_ref, codecol_ref, start_ref,
     gi_ref, ginj_ref, gread_ref, gw_ref, rate_out,
     cot, wslot, acc, own, part_send, part_recv, plane_send, plane_recv, zsend, zrecv,
     fwd_t, mix_t, wts, wts_t, qts, scal, inc, chain_send, rate_z, rate_dp, rate_mine, rate_mid,
@@ -143,7 +143,7 @@
     lower = row_at >= col_at
     upper = col_at >= row_at
     col_sum = nn(jnp.where(lower, 1.0, 0.0).astype(BF16), codecol_ref[...])
-    row_sum = nn(coderow_ref[...], jnp.where(upper, 1.0, 0.0).astype(BF16))
+    row_sum = col_sum.T
     inter_t = nt(inj_ref[...], read_ref[...])
     x_t = x_ref[...].astype(F32).T.astype(BF16)
     cum_col, cum_row = [], []
@@ -169,24 +169,53 @@
         at = pl.ds(pl.multiple_of((chip_at * 2 + core_at) * cols, cols), cols)
         return nn(fwd_t[...], cot[:, at])
 
-    order = list(range(1, chips)) + [0]
-    for i in order:
-        target = lax.rem(chip + i, chips)
-        part_send[i] = block(target, 1 - core).astype(BF16)
-        send(part_send.at[i], part_recv.at[i], asem.at[i], partner)
+    levels = chips.bit_length() - 1
+    bits = [lax.rem(lax.div(chip, 1 << k), 2) for k in range(levels)]
+
+    def chip_across(offset):
+        return chip + sum(((1 << k) * (1 - 2 * bits[k]) for k in range(levels) if offset >> k & 1), 0)
+
+    half = fwd_t.shape[0] // 2
+    ways = (list(range(levels)), list(range(levels))[::-1])
+
+    def leaving(way, level):
+        keys = ways[way]
+        return [r for r in range(chips) if r >> keys[level] & 1 and not any(r >> keys[k] & 1 for k in range(level))]
+
+    def plane_out(way, level, r):
+        bit_at = 1 << ways[way][level]
+        at = slice(way * half, (way + 1) * half)
+        plane_send[way, r - 1] = own[r, at].astype(BF16)
+        send(plane_send.at[way, r - 1], plane_recv.at[way, r - 1], bsem.at[way, r - 1],
+             (chip_across(bit_at) * 2 + core, c))
+
+    def plane_in(level):
+        for way in range(2):
+            bit_at = 1 << ways[way][level]
+            at = slice(way * half, (way + 1) * half)
+            for r in leaving(way, level):
+                arrived(plane_recv.at[way, r - 1], bsem.at[way, r - 1])
+                own[r - bit_at, at] = own[r - bit_at, at] + plane_recv[way, r - 1].astype(F32)
+            if level + 1 < levels:
+                for r in leaving(way, level + 1):
+                    plane_out(way, level + 1, r)
+
+    first = [r for r in range(1, chips) if r & 1 and r >> (levels - 1) & 1]
+    order = first + [r for r in range(chips - 1, -1, -1) if r not in first]
+    for r in order:
+        part_send[r] = block(chip_across(r), 1 - core).astype(BF16)
+        send(part_send.at[r], part_recv.at[r], asem.at[r], partner)
     w_z(0)
-    for i in order:
-        target = lax.rem(chip + i, chips)
-        own[i] = block(target, core)
-        arrived(part_recv.at[i], asem.at[i])
-        if i:
-            plane_send[i - 1] = (own[i] + part_recv[i].astype(F32)).astype(BF16)
-            send(plane_send.at[i - 1], plane_recv.at[i - 1], bsem.at[i - 1], (target * 2 + core, c))
-        else:
-            own[0] = own[0] + part_recv[0].astype(F32)
-
+    for r in order:
+        mine_too = block(chip_across(r), core)
+        arrived(part_recv.at[r], asem.at[r])
+        own[r] = mine_too + part_recv[r].astype(F32)
+        for way in range(2):
+            if r in leaving(way, 0):
+                plane_out(way, 0, r)
+
+    w_plane(0)
     acc[...] = nt(cot[:, pl.ds(pl.multiple_of(c * dz, dz), dz)], w_ref[...])
-    w_plane(0)
     for step in range(1, n - 1):
         w_z(step)
         if step == 1:
@@ -199,8 +228,16 @@
                 high, low = halves(jnp.exp(cum_col[h]) * read_ref[...].astype(F32))
                 scal[h, :, :128] = high
                 scal[h, :, 128:] = low
+            for level in range(levels - 1):
+                plane_in(level)
         w_use(step - 1)
         w_plane(step)
+    plane_in(levels - 1)
+    for i in range(1, n):
+        target = lax.rem(c + i, n)
+        at = pl.ds(pl.multiple_of(target * rows, rows), rows)
+        zsend[i - 1] = own[0, at, :].astype(BF16)
+        send(zsend.at[i - 1], zrecv.at[i - 1], dsem.at[i - 1], (dp, target))
     w_use(n - 2)
 
     grad = acc[...].astype(BF16)
@@ -251,15 +288,6 @@
 
         send(chain_send.at[h], inc.at[h], chsem.at[h], before, (c < n - 1) & (c > 0))
 
-    for i in range(chips - 1):
-        arrived(plane_recv.at[i], bsem.at[i])
-        own[0] = own[0] + plane_recv[i].astype(F32)
-    for i in range(1, n):
-        target = lax.rem(c + i, n)
-        at = pl.ds(pl.multiple_of(target * rows, rows), rows)
-        zsend[i - 1] = own[0, at, :].astype(BF16)
-        send(zsend.at[i - 1], zrecv.at[i - 1], dsem.at[i - 1], (dp, target))
-
     rate_mine[...] = jnp.zeros_like(rate_mine)
     ginj = ginj_ref[...]
     for h in range(heads):
@@ -296,13 +324,22 @@
     for i in range(dps - 1):
         arrived(rate_dp.at[i], r2sem.at[i])
         total = total + rate_dp[i]
-    rate_out[...] = total
+    whole = jnp.sum(total, axis=1, keepdims=True) / (length * dps * n)
+    rate_out[...] = jnp.broadcast_to(whole, rate_out.shape)
 
     for copy, cond in sent:
         if cond is None:
             copy.wait_send()
         else:
             pl.when(cond)(lambda: copy.wait_send())
+
+
+def hand_over(*refs):
+    copies = [pltpu.make_async_copy(refs[i], refs[4 + i], refs[8].at[i]) for i in range(4)]
+    for copy in copies:
+        copy.start()
+    for copy in copies:
+        copy.wait()
 
 
 def local(n, dps, cotangent, out_weight, head_input, injector, readout, decay_code, decay_rate, start_state):
@@ -314,8 +351,7 @@
     code = decay_code[0]
     parts = jnp.concatenate([code // 256, code % 256], axis=1).astype(BF16)
     code_col = jnp.pad(parts, ((0, 0), (0, 128 - 2 * heads)))
-    code_row = jnp.pad(parts.T, ((0, 16 - 2 * heads), (0, 0)))
-    sends = 2 + 2 * (n - 2) + 6 * (n - 1) + chips + (chips - 1) + 2 * heads + 2 * (n - 1) + (dps - 1)
+    sends = 2 + 2 * (n - 2) + 6 * (n - 1) + chips + 2 * (chips - 1) + 2 * heads + 2 * (n - 1) + (dps - 1)
     vmem = pl.BlockSpec(memory_space=pltpu.VMEM)
     dma = pltpu.SemaphoreType.DMA
     gi, ginj, gread, gw, rate = pl.pallas_call(
@@ -327,7 +363,7 @@
             jax.ShapeDtypeStruct((rows, cols), F32),
             jax.ShapeDtypeStruct((8, 128), F32),
         ),
-        in_specs=[pl.BlockSpec(memory_space=pltpu.SMEM), pl.BlockSpec(memory_space=pl.ANY)] + [vmem] * 7,
+        in_specs=[pl.BlockSpec(memory_space=pltpu.SMEM), pl.BlockSpec(memory_space=pl.ANY)] + [vmem] * 6,
         out_specs=(vmem,) * 5,
         scratch_shapes=[
             pltpu.VMEM((length, width), BF16),
@@ -336,8 +372,8 @@
             pltpu.VMEM((chips, channels, cols), F32),
             pltpu.VMEM((chips, channels, cols), BF16),
             pltpu.VMEM((chips, channels, cols), BF16),
-            pltpu.VMEM((chips - 1, channels, cols), BF16),
-            pltpu.VMEM((chips - 1, channels, cols), BF16),
+            pltpu.VMEM((2, chips - 1, channels // 2, cols), BF16),
+            pltpu.VMEM((2, chips - 1, channels // 2, cols), BF16),
             pltpu.VMEM((n - 1, rows, cols), BF16),
             pltpu.VMEM((n - 1, rows, cols), BF16),
             pltpu.VMEM((channels, length), BF16),
@@ -358,7 +394,7 @@
             dma((2, n - 1)),
             dma((2, n - 1, 2)),
             dma((chips,)),
-            dma((chips - 1,)),
+            dma((2, chips - 1)),
             dma((n - 1,)),
             dma((heads,)),
             dma((n - 1,)),
@@ -370,10 +406,18 @@
         cost_estimate=pl.CostEstimate(flops=10**10, bytes_accessed=2 * 10**7, transcendentals=10**6),
     )(
         decay_rate, cotangent[0], out_weight, head_input[0], injector[0], readout[0],
-        code_col, code_row, start_state[0, 0],
+        code_col, start_state[0, 0],
     )
-    tokens_all = length * dps * n
-    return gi[None], ginj[None], gread[None], gw, jnp.sum(rate, axis=1)[:heads] / tokens_all
+    anywhere = pl.BlockSpec(memory_space=pl.ANY)
+    results = (gi, ginj, gread, gw)
+    gi, ginj, gread, gw = pl.pallas_call(
+        hand_over,
+        out_shape=tuple(jax.ShapeDtypeStruct(part.shape, part.dtype) for part in results),
+        in_specs=[anywhere] * 4,
+        out_specs=(anywhere,) * 4,
+        scratch_shapes=[dma((4,))],
+    )(*results)
+    return gi[None], ginj[None], gread[None], gw, rate[:heads, 0]
 
 
 def solution(mesh):

time: 98.2 us -> 106 us (1.079)
  Pallas kernels: 87 us -> 102 us
  local copies, waits for them, and re-layouts: 8.15 us -> 2.17 us
  other arithmetic: 2.03 us -> 0.72 us
    pallas_call x0 -> x1, Pallas kernels: none -> 32.9 us  [local(): pl.pallas_call(hand_over, out_shape=tuple((jax.ShapeDtypeStruct(part.shap...]
    pallas_call x1, Pallas kernels: 87 us -> 69 us  [local(): pl.pallas_call(functools.partial(kernel, n, dps), out_shape=(jax.ShapeDty...]
    unnamed x5 -> x0, local copies, waits for them, and re-layouts: 6.85 us -> none
    slice x0 -> x1, local copies, waits for them, and re-layouts: none -> 1.31 us  [local(): return (gi[None], ginj[None], gread[None], gw, rate[:heads, 0])]
where the time goes in v2:
time: 106 us; the launch traced here: 105 us
  Pallas kernels  102 us (96%)
  local copies, waits for them, and re-layouts  2.17 us (2%)
    pallas_call x1, Pallas kernels, local(): pl.pallas_call(functools.partial(kernel, n, dps), out_shape=(jax.ShapeDty...  69 us
    pallas_call x1, Pallas kernels, local(): pl.pallas_call(hand_over, out_shape=tuple((jax.ShapeDtypeStruct(part.shap...  32.9 us

profile of v2, /device:TPU:9, one launch (start us, length us, event | category | flops | bytes accessed | tf_op | source)
XLA Modules:
  0.0 105.4 jit_solution(14061241657421140921)
XLA Ops:
  0.6 0.7 fusion.1
  1.4 0.2 copy.15
  1.5 0.7 pad.4.codecol_ref
  2.2 69.0 %shard_map.119 = (bf16[512,256]{1,0:T(8,128)(2,1)}, f32[512,128]{1,0:T(8,128)}, f32[512,128]{1,0:T(8,128)}, f32[64,1024]{1,0:T(8,128)}, f32[8,128]{1,0:T(8,128)}) custom-call(f32[2]{0:T(128)} %rate_ref.1, bf16[512,8192]{1,0:T(8,128)(2,1)} %bitcast.30, bf16[256,2048]{1,0:T(8,128)(2,1)} %w_ref.1, bf16[512,256]{1,0:T(8,128)(2,1)} %bitcast.31, ...), custom_call_target="tpu_custom_call" | custom-call | flops 10000000000 | bytes 20000000 | tf_op jit(solution)/shard_map/pallas_call | solution.py:357
  71.2 32.9 %shard_map.120 = (bf16[512,256]{1,0:T(8,128)(2,1)}, f32[512,128]{1,0:T(8,128)}, f32[512,128]{1,0:T(8,128)}, f32[64,1024]{1,0:T(8,128)}) custom-call(bf16[512,256]{1,0:T(8,128)(2,1)} %get-tuple-element.14.refs_0_, f32[512,128]{1,0:T(8,128)} %get-tuple-element.15.refs_1_, f32[512,128]{1,0:T(8,128)} %get-tuple-element.16.refs_2_, ...), custom_call_target="tpu_custom_call" | custom-call | tf_op jit(solution)/shard_map/pallas_call | solution.py:413
  104.1 1.3 %slice_reduce_fusion = f32[2]{0:T(128)} fusion(f32[8,128]{1,0:T(8,128)} %get-tuple-element.22), kind=kLoop, calls=%fused_computation.11 | loop fusion | bytes 16 | tf_op jit(solution)/shard_map/slice | solution.py:420
  (1 shorter events, 0.0 us)

commit v3 on v2

--- a/solution.py
+++ b/solution.py
@@ -228,16 +228,12 @@
                 high, low = halves(jnp.exp(cum_col[h]) * read_ref[...].astype(F32))
                 scal[h, :, :128] = high
                 scal[h, :, 128:] = low
-            for level in range(levels - 1):
-                plane_in(level)
+        if step < n - 2:
+            w_plane(step)
         w_use(step - 1)
-        w_plane(step)
-    plane_in(levels - 1)
-    for i in range(1, n):
-        target = lax.rem(c + i, n)
-        at = pl.ds(pl.multiple_of(target * rows, rows), rows)
-        zsend[i - 1] = own[0, at, :].astype(BF16)
-        send(zsend.at[i - 1], zrecv.at[i - 1], dsem.at[i - 1], (dp, target))
+    for level in range(levels - 1):
+        plane_in(level)
+    w_plane(n - 2)
     w_use(n - 2)
 
     grad = acc[...].astype(BF16)
@@ -276,6 +272,15 @@
         rates.append(rate_row)
     gread_ref[...] = nn(pair.astype(BF16), inject) + through_sum
     ginj_ref[...] = nn(pair_t.astype(BF16), read)
+    for h in range(heads):
+        ch = slice(h * 128, (h + 1) * 128)
+        acc[:, ch] = nn(mix_t[h], grad[:, ch])
+    plane_in(levels - 1)
+    for i in range(1, n):
+        target = lax.rem(c + i, n)
+        at = pl.ds(pl.multiple_of(target * rows, rows), rows)
+        zsend[i - 1] = own[0, at, :].astype(BF16)
+        send(zsend.at[i - 1], zrecv.at[i - 1], dsem.at[i - 1], (dp, target))
 
     for h in range(heads):
         @pl.when(c < n - 1)
@@ -289,23 +294,23 @@
         send(chain_send.at[h], inc.at[h], chsem.at[h], before, (c < n - 1) & (c > 0))
 
     rate_mine[...] = jnp.zeros_like(rate_mine)
-    ginj = ginj_ref[...]
+    reached = []
     for h in range(heads):
         ch = slice(h * 128, (h + 1) * 128)
         left = last[h] - cum_col[h]
-        to_end = jnp.exp(left)
         high, low = halves(inc[h])
-        entering = to_end * nt(inject, high)
-        gi_ref[:, ch] = (nn(mix_t[h], grad[:, ch]) + entering).astype(BF16)
-        reach = to_end * (nn(x_ref[:, ch], high) + nn(x_ref[:, ch], low))
-        ginj = ginj + reach
+        reach = jnp.exp(left) * (nn(x_ref[:, ch], high) + nn(x_ref[:, ch], low))
+        reached.append(reach)
         row = rates[h] + jnp.sum(left * (reach * inject.astype(F32)), axis=0, keepdims=True)
         row = row + (jnp.exp(last[h]) * last[h]) * jnp.sum(inc[h] * start_ref[h], axis=0, keepdims=True)
         rate_mine[h : h + 1, :] = row
-    ginj_ref[...] = ginj
-
     for i in range(1, n):
         send(rate_mine, rate_z.at[i - 1], r1sem.at[i - 1], (dp, lax.rem(c + i, n)))
+    ginj_ref[...] = ginj_ref[...] + sum(reached[1:], reached[0])
+    for h in range(heads):
+        ch = slice(h * 128, (h + 1) * 128)
+        entering = jnp.exp(last[h] - cum_col[h]) * nt(inject, inc[h].astype(BF16))
+        gi_ref[:, ch] = (acc[:, ch] + entering).astype(BF16)
     total = rate_mine[...]
     for i in range(n - 1):
         arrived(rate_z.at[i], r1sem.at[i])
@@ -335,11 +340,8 @@
 
 
 def hand_over(*refs):
-    copies = [pltpu.make_async_copy(refs[i], refs[4 + i], refs[8].at[i]) for i in range(4)]
-    for copy in copies:
-        copy.start()
-    for copy in copies:
-        copy.wait()
+    for i in range(4):
+        refs[4 + i][...] = refs[i][...]
 
 
 def local(n, dps, cotangent, out_weight, head_input, injector, readout, decay_code, decay_rate, start_state):
@@ -408,14 +410,12 @@
         decay_rate, cotangent[0], out_weight, head_input[0], injector[0], readout[0],
         code_col, start_state[0, 0],
     )
-    anywhere = pl.BlockSpec(memory_space=pl.ANY)
     results = (gi, ginj, gread, gw)
     gi, ginj, gread, gw = pl.pallas_call(
         hand_over,
         out_shape=tuple(jax.ShapeDtypeStruct(part.shape, part.dtype) for part in results),
-        in_specs=[anywhere] * 4,
-        out_specs=(anywhere,) * 4,
-        scratch_shapes=[dma((4,))],
+        in_specs=[vmem] * 4,
+        out_specs=(vmem,) * 4,
     )(*results)
     return gi[None], ginj[None], gread[None], gw, rate[:heads, 0]
 

time: 106 us -> 75.7 us (0.71)
  Pallas kernels: 102 us -> 71.9 us
    pallas_call x1, Pallas kernels: 32.9 us -> 2.17 us  [local(): pl.pallas_call(hand_over, out_shape=tuple((jax.ShapeDtypeStruct(part.shap...]
where the time goes in v3:
time: 75.7 us; the launch traced here: 75.5 us
  Pallas kernels  71.9 us (95%)
  local copies, waits for them, and re-layouts  2.17 us (3%)
    pallas_call x1, Pallas kernels, local(): pl.pallas_call(functools.partial(kernel, n, dps), out_shape=(jax.ShapeDty...  69.8 us
    pallas_call x1, Pallas kernels, local(): pl.pallas_call(hand_over, out_shape=tuple((jax.ShapeDtypeStruct(part.shap...  2.17 us

profile of v3, /device:TPU:9, one launch (start us, length us, event | category | flops | bytes accessed | tf_op | source)
XLA Modules:
  0.0 75.5 jit_solution(11883211535484552575)
XLA Ops:
  0.6 0.7 fusion.1
  1.4 0.2 copy.15
  1.5 0.7 pad.4.codecol_ref
  2.2 69.8 %shard_map.119 = (bf16[512,256]{1,0:T(8,128)(2,1)}, f32[512,128]{1,0:T(8,128)}, f32[512,128]{1,0:T(8,128)}, f32[64,1024]{1,0:T(8,128)}, f32[8,128]{1,0:T(8,128)}) custom-call(f32[2]{0:T(128)} %rate_ref.1, bf16[512,8192]{1,0:T(8,128)(2,1)} %bitcast.30, bf16[256,2048]{1,0:T(8,128)(2,1)} %w_ref.1, bf16[512,256]{1,0:T(8,128)(2,1)} %bitcast.31, ...), custom_call_target="tpu_custom_call" | custom-call | flops 10000000000 | bytes 20000000 | tf_op jit(solution)/shard_map/pallas_call | solution.py:359
  72.0 2.2 %shard_map.120 = (bf16[512,256]{1,0:T(8,128)(2,1)}, f32[512,128]{1,0:T(8,128)}, f32[512,128]{1,0:T(8,128)}, f32[64,1024]{1,0:T(8,128)}) custom-call(bf16[512,256]{1,0:T(8,128)(2,1)} %get-tuple-element.14.refs_0_, f32[512,128]{1,0:T(8,128)} %get-tuple-element.15.refs_1_, f32[512,128]{1,0:T(8,128)} %get-tuple-element.16.refs_2_, ...), custom_call_target="tpu_custom_call" | custom-call | tf_op jit(solution)/shard_map/pallas_call | solution.py:414
  74.2 1.3 %slice_reduce_fusion = f32[2]{0:T(128)} fusion(f32[8,128]{1,0:T(8,128)} %get-tuple-element.22), kind=kLoop, calls=%fused_computation.11 | loop fusion | bytes 16 | tf_op jit(solution)/shard_map/slice | solution.py:420
  (1 shorter events, 0.0 us)

commit v4 on v3

--- a/solution.py
+++ b/solution.py
@@ -214,11 +214,12 @@
             if r in leaving(way, 0):
                 plane_out(way, 0, r)
 
-    w_plane(0)
-    acc[...] = nt(cot[:, pl.ds(pl.multiple_of(c * dz, dz), dz)], w_ref[...])
+    own_product = lambda: nt(cot[:, pl.ds(pl.multiple_of(c * dz, dz), dz)], w_ref[...])
     for step in range(1, n - 1):
         w_z(step)
+        w_plane(step - 1)
         if step == 1:
+            acc[...] = own_product()
             inter = nt(read_ref[...], inj_ref[...])
             for h in range(heads):
                 spread = jnp.where(lower, cum_col[h] - cum_row[h], 0.0)
@@ -228,9 +229,9 @@
                 high, low = halves(jnp.exp(cum_col[h]) * read_ref[...].astype(F32))
                 scal[h, :, :128] = high
                 scal[h, :, 128:] = low
-        if step < n - 2:
-            w_plane(step)
-        w_use(step - 1)
+        else:
+            w_use(step - 2)
+    w_use(n - 3)
     for level in range(levels - 1):
         plane_in(level)
     w_plane(n - 2)
@@ -341,7 +342,9 @@
 
 def hand_over(*refs):
     for i in range(4):
-        refs[4 + i][...] = refs[i][...]
+        refs[5 + i][...] = refs[i][...]
+    for h in range(refs[9].shape[0]):
+        refs[9][h] = refs[4][h, 0]
 
 
 def local(n, dps, cotangent, out_weight, head_input, injector, readout, decay_code, decay_rate, start_state):
@@ -410,14 +413,16 @@
         decay_rate, cotangent[0], out_weight, head_input[0], injector[0], readout[0],
         code_col, start_state[0, 0],
     )
+    smem = pl.BlockSpec(memory_space=pltpu.SMEM)
     results = (gi, ginj, gread, gw)
-    gi, ginj, gread, gw = pl.pallas_call(
+    gi, ginj, gread, gw, rate = pl.pallas_call(
         hand_over,
-        out_shape=tuple(jax.ShapeDtypeStruct(part.shape, part.dtype) for part in results),
-        in_specs=[vmem] * 4,
-        out_specs=(vmem,) * 4,
-    )(*results)
-    return gi[None], ginj[None], gread[None], gw, rate[:heads, 0]
+        out_shape=tuple(jax.ShapeDtypeStruct(part.shape, part.dtype) for part in results)
+        + (jax.ShapeDtypeStruct((heads,), F32),),
+        in_specs=[vmem] * 4 + [smem],
+        out_specs=(vmem,) * 4 + (smem,),
+    )(*results, rate)
+    return gi[None], ginj[None], gread[None], gw, rate
 
 
 def solution(mesh):

time: 75.7 us -> 73.8 us (0.975)
  local copies, waits for them, and re-layouts: 2.17 us -> 0.86 us
    slice x1 -> x0, local copies, waits for them, and re-layouts: 1.3 us -> none  [local(): return (gi[None], ginj[None], gread[None], gw, rate[:heads, 0])]
where the time goes in v4:
time: 73.8 us; the launch traced here: 73.6 us
  Pallas kernels  71.3 us (97%)
  local copies, waits for them, and re-layouts  0.86 us (1%)
    pallas_call x1, Pallas kernels, local(): pl.pallas_call(functools.partial(kernel, n, dps), out_shape=(jax.ShapeDty...  69.1 us
    pallas_call x1, Pallas kernels, local(): pl.pallas_call(hand_over, out_shape=tuple((jax.ShapeDtypeStruct(part.shap...  2.19 us

profile of v4, /device:TPU:9, one launch (start us, length us, event | category | flops | bytes accessed | tf_op | source)
XLA Modules:
  0.0 73.6 jit_solution(832205139356925686)
XLA Ops:
  0.6 0.7 fusion.1
  1.4 0.2 copy.14
  1.5 0.7 pad.4.codecol_ref
  2.2 69.1 %shard_map.119 = (bf16[512,256]{1,0:T(8,128)(2,1)}, f32[512,128]{1,0:T(8,128)}, f32[512,128]{1,0:T(8,128)}, f32[64,1024]{1,0:T(8,128)}, f32[8,128]{1,0:T(8,128)}) custom-call(f32[2]{0:T(128)} %rate_ref.1, bf16[512,8192]{1,0:T(8,128)(2,1)} %bitcast.30, bf16[256,2048]{1,0:T(8,128)(2,1)} %w_ref.1, bf16[512,256]{1,0:T(8,128)(2,1)} %bitcast.31, ...), custom_call_target="tpu_custom_call" | custom-call | flops 10000000000 | bytes 20000000 | tf_op jit(solution)/shard_map/pallas_call | solution.py:362
  71.4 2.2 %shard_map.120 = (bf16[512,256]{1,0:T(8,128)(2,1)}, f32[512,128]{1,0:T(8,128)}, f32[512,128]{1,0:T(8,128)}, f32[64,1024]{1,0:T(8,128)}, f32[2]{0:T(128)}) custom-call(bf16[512,256]{1,0:T(8,128)(2,1)} %get-tuple-element.15.refs_0_, f32[512,128]{1,0:T(8,128)} %get-tuple-element.16.refs_1_, f32[512,128]{1,0:T(8,128)} %get-tuple-element.17.refs_2_, ...), custom_call_target="tpu_custom_call" | custom-call | tf_op jit(solution)/shard_map/pallas_call | solution.py:418
  (1 shorter events, 0.0 us)
